TPU v7x, 32 devices: a whole 2x2x4 slice. The times are simulated.
32 devices in a mesh: lat: 4 (over y, core), lon: 8 (over z, x).
Axes of the slice: x: 2, y: 2, z: 4, core: 2. Of those that a mesh axis runs over, the one named last changes fastest.
Arguments:
- source_elements: bfloat16 [16384, 256], P(('lat', 'lon')), may hold values from -6 to 6
- remap_weights: bfloat16 [32, 32, 6, 16, 128], P(('lat', 'lon')), may hold values from -1.5 to 1.5
- element_index: int32 [32, 32, 6], P(('lat', 'lon')), may hold values from 0 to 511
- patch_index: int32 [32, 32, 6], P(('lat', 'lon')), may hold values from 0 to 127
- block_counts: int32 [32, 32], P(('lat', 'lon')), may hold values from 2 to 6, as said below
- conv_weight: bfloat16 [9, 64, 16], replicated, may hold values from -0.5 to 0.5
- cotangent: bfloat16 [64, 64, 8192], P('lat', None, 'lon'), may hold values from -6 to 6
Outputs:
- features_out: bfloat16 [64, 64, 8192], P('lat', None, 'lon')
- input_grad: bfloat16 [64, 16, 8192], P('lat', None, 'lon')
- weight_grad: float32 [9, 64, 16], replicated
Inputs may be any that keep to these rules, and one draw needn't show every extreme that they name: `block_counts`: at most 6 valid slots from one device to one owner; in every draw one owner, drawn from the seed, receives exactly 6 from every device.
All inputs are finite; a program needn't handle non-finite values.
Results may differ from a plain program's by a relative error of at most 0.0058.
Values may be sent and summed in bfloat16 or wider, within the bound.
A program may use at most 128 MiB of HBM per device.

v0:
```python
import math

import jax
import jax.numpy as jnp
from jax import lax
from jax.sharding import PartitionSpec as P

RATE = 4


def extended(block, sides, width, periodic):
    for axis, dim in sides:
        count = lax.axis_size(axis)
        forward = [(i, i + 1) for i in range(count - 1)]
        if periodic:
            forward.append((count - 1, 0))
        backward = [(target, source) for source, target in forward]
        low = lax.ppermute(
            lax.slice_in_dim(block, block.shape[dim] - width, None, axis=dim), axis, forward
        )
        high = lax.ppermute(lax.slice_in_dim(block, 0, width, axis=dim), axis, backward)
        block = jnp.concatenate([low, block, high], axis=dim)
    return block


def tap_offsets():
    return [((tap_number // 3 - 1) * RATE, (tap_number % 3 - 1) * RATE) for tap_number in range(9)]


def route(payload, targets):
    arrived, arrived_targets = (
        lax.all_to_all(payload, ("lat", "lon"), split_axis=0, concat_axis=0, tiled=True),
        lax.all_to_all(targets, ("lat", "lon"), split_axis=0, concat_axis=0, tiled=True),
    )
    return (arrived, arrived_targets)


def local(
    source_elements, remap_weights, element_index, patch_index, block_counts, conv_weight, cotangent
):
    local_weights = remap_weights[0]
    chosen = element_index[0]
    targets = patch_index[0]
    counts = block_counts[0]
    owners, capacity, points, patch_cells = local_weights.shape
    out_channels = conv_weight.shape[1]
    variables = conv_weight.shape[2]
    band_rows = cotangent.shape[0]
    band_cols = cotangent.shape[2]
    live_slots = jnp.arange(capacity, dtype=jnp.int32)[None, :] < counts[:, None]
    element_rows = source_elements[chosen].reshape(owners, capacity, points, variables)
    blocks = jnp.einsum(
        "dkjc,dkjp->dkcp", element_rows, local_weights, preferred_element_type=jnp.float32
    )
    blocks = jnp.where(live_slots[:, :, None, None], blocks, 0.0).astype(jnp.bfloat16)
    arrived, arrived_targets = route(
        blocks.reshape(owners, capacity, variables * patch_cells), targets
    )
    contributions = arrived.reshape(owners, capacity, variables, patch_cells).astype(jnp.float32)
    patch_total = band_rows * band_cols // patch_cells
    summed = jax.ops.segment_sum(
        contributions.reshape(owners * capacity, variables, patch_cells),
        arrived_targets.reshape(owners * capacity),
        num_segments=patch_total,
    )
    remapped = summed.reshape(
        band_rows, band_cols // patch_cells, variables, patch_cells
    ).transpose(0, 2, 1, 3)
    remapped = remapped.reshape(band_rows, variables, band_cols).astype(jnp.bfloat16)
    stacked = jnp.concatenate([remapped, cotangent], axis=1)
    beside_all = extended(stacked, (("lon", 2),), RATE, True)
    beside_all = extended(beside_all, (("lat", 0),), RATE, False)
    padded_x = beside_all[:, :variables]
    padded_g = beside_all[:, variables:]
    forward = jnp.zeros((band_rows, out_channels, band_cols), jnp.float32)
    backward = jnp.zeros((band_rows, variables, band_cols), jnp.float32)
    partials = []
    for tap_number, (row_shift, col_shift) in enumerate(tap_offsets()):
        shifted = padded_x[
            RATE + row_shift : RATE + row_shift + band_rows,
            :,
            RATE + col_shift : RATE + col_shift + band_cols,
        ]
        forward = forward + jnp.einsum(
            "oc,rcw->row", conv_weight[tap_number], shifted, preferred_element_type=jnp.float32
        )
        back_piece = padded_g[
            RATE - row_shift : RATE - row_shift + band_rows,
            :,
            RATE - col_shift : RATE - col_shift + band_cols,
        ]
        backward = backward + jnp.einsum(
            "oc,row->rcw", conv_weight[tap_number], back_piece, preferred_element_type=jnp.float32
        )
        partials.append(
            jnp.einsum("row,rcw->oc", cotangent, shifted, preferred_element_type=jnp.float32)
        )
    local_grad = jnp.stack(partials)
    total_grad = lax.psum(local_grad, ("lat", "lon"))
    cell_total = band_rows * band_cols * lax.axis_size("lat") * lax.axis_size("lon")
    return (
        forward.astype(jnp.bfloat16),
        backward.astype(jnp.bfloat16),
        total_grad / math.sqrt(cell_total),
    )


def solution(mesh):
    in_specs = (
        P(("lat", "lon"), None),
        P(("lat", "lon"), None, None, None, None),
        P(("lat", "lon"), None, None),
        P(("lat", "lon"), None, None),
        P(("lat", "lon"), None),
        P(),
        P("lat", None, "lon"),
    )
    out_specs = (P("lat", None, "lon"), P("lat", None, "lon"), P())
    return jax.shard_map(local, mesh=mesh, in_specs=in_specs, out_specs=out_specs, check_vma=False)
```

profile of v0, /device:TPU:0, one launch (start us, length us, event | category | flops | bytes accessed | tf_op | source)
XLA Modules:
  0.0 205.1 jit_solution(11412642652437973795)
XLA Ops:
  2.1 7.3 %all-to-all-start = ((s32[32,1,6]{2,1,0:T(1,128)}), s32[32,1,6]{2,1,0:T(1,128)S(1)}, u32[]{:S(2)}, u32[]{:S(2)}) async-start(s32[32,1,6]{2,1,0:T(1,128)} %copy.29), calls=%async_computation | async-start | bytes 32768 | tf_op jit(solution)/shard_map/all_to_all | solution.py:33
  11.0 1.9 gather_fusion
  14.3 2.8 %select_convert_fusion = bf16[32,6,16,128]{3,2,1,0:T(8,128)(2,1)} fusion(bf16[32,6,16,16]{3,2,1,0:T(8,128)(2,1)} %reshape.79, bf16[1,32,6,16,128]{4,3,2,1,0:T(8,128)(2,1)S(1)} %copy-done, pred[32,6]{1,0:T(8,128)(4,1)S(1)} %iota_compare_fusion), kind=kOutput, calls=%fused_computation.32 | convolution fusion | flops 13369344 | bytes 1671360 | tf_op jit(solution)/shard_map/dkjc,dkjp->dkcp/dot_general | solution.py:52
  17.1 2.7 %reshape.119 = bf16[32,6,2048]{2,1,0:T(8,128)(2,1)} reshape(bf16[32,6,16,128]{3,2,1,0:T(8,128)(2,1)} %select_convert_fusion) | data formatting | bytes 1572864 | tf_op jit(solution)/shard_map/reshape | solution.py:57
  19.7 6.0 %all-to-all-start.1 = ((bf16[32,6,2048]{2,1,0:T(8,128)(2,1)}), bf16[32,6,2048]{2,1,0:T(8,128)(2,1)}, u32[]{:S(2)}, u32[]{:S(2)}) async-start(bf16[32,6,2048]{2,1,0:T(8,128)(2,1)} %reshape.119), calls=%async_computation.1 | async-start | bytes 2097152 | tf_op jit(solution)/shard_map/all_to_all | solution.py:32
  25.7 2.1 %fusion.68 = f32[16,1024,16]{1,2,0:T(8,128)} fusion(bf16[16,64,1024]{2,1,0:T(8,128)(2,1)S(1)} %copy-done.2, bf16[9,64,16]{1,2,0:T(8,128)(2,1)} %param.12), kind=kOutput, calls=%fused_computation.93 | convolution fusion | flops 33554432 | bytes 3149824 | tf_op jit(solution)/shard_map/oc,row->rcw/dot_general | solution.py:92
  29.1 24.2 %all-to-all-done.1 = bf16[32,6,2048]{2,1,0:T(8,128)(2,1)} async-done(((bf16[32,6,2048]{2,1,0:T(8,128)(2,1)}), bf16[32,6,2048]{2,1,0:T(8,128)(2,1)}, u32[]{:S(2)}, u32[]{:S(2)}) %all-to-all-start.1) | async-done | bytes 786464 | tf_op jit(solution)/shard_map/all_to_all | solution.py:32
  53.3 2.8 %reshape.94 = f32[192,16,128]{2,1,0:T(8,128)} reshape(bf16[32,6,2048]{2,1,0:T(8,128)(2,1)} %all-to-all-done.1) | data formatting | bytes 2359296 | tf_op jit(solution)/shard_map/convert_element_type | solution.py:59
  57.1 23.9 %scatter_fusion = f32[128,16,128]{2,1,0:T(8,128)} fusion(f32[128,16,128]{2,1,0:T(8,128)} %broadcast_in_dim.18, s32[192]{0:T(256)S(1)} %reshape.92, f32[192,16,128]{2,1,0:T(8,128)} %reshape.94), kind=kCustom, calls=%fused_computation.1 | custom fusion | flops 393216 | bytes 4719360 | tf_op jit(solution)/shard_map/scatter-add | solution.py:61
  84.9 2.7 %fusion.50 = f32[16,1024,64]{1,2,0:T(8,128)} fusion(bf16[16,8,2,8,128]{4,3,2,1,0:T(8,128)(2,1)S(1)} %bitcast.181, bf16[9,64,16]{1,2,0:T(8,128)(2,1)S(1)} %copy-done.16), kind=kOutput, calls=%fused_computation.63 | convolution fusion | flops 33554432 | bytes 4722688 | tf_op jit(solution)/shard_map/oc,rcw->row/dot_general | solution.py:84
  87.6 11.6 %collective-permute-done.1 = bf16[16,80,4]{2,1,0:T(8,128)(2,1)S(1)} collective-permute-done((bf16[16,80,4]{2,1,0:T(8,128)(2,1)S(1)}, bf16[16,80,4]{2,1,0:T(8,128)(2,1)S(1)}, u32[]{:S(2)}, u32[]{:S(2)}) %collective-permute-start.1) | collective-permute-done | bytes 10272 | tf_op jit(solution)/shard_map/ppermute | solution.py:21
  99.2 6.8 %concatenate.32 = bf16[16,80,1032]{2,1,0:T(8,128)(2,1)} concatenate(bf16[16,80,4]{2,1,0:T(8,128)(2,1)S(1)} %collective-permute-done, bf16[16,80,1024]{2,1,0:T(8,128)(2,1)} %copy-done.5, bf16[16,80,4]{2,1,0:T(8,128)(2,1)S(1)} %collective-permute-done.1), dimensions={2} | concatenate | bytes 5283840 | tf_op jit(solution)/shard_map/concatenate | solution.py:22
  110.4 1.8 fusion.17
  112.7 2.8 %fusion.66 = f32[16,1024,64]{1,2,0:T(8,128)} fusion(bf16[16,16,1024]{2,1,0:T(8,128)(2,1)S(1)} %get-tuple-element.15, bf16[9,64,16]{1,2,0:T(8,128)(2,1)S(1)} %copy-done.16), kind=kOutput, calls=%fused_computation.91 | convolution fusion | flops 33554432 | bytes 4722688 | tf_op jit(solution)/shard_map/oc,rcw->row/dot_general | solution.py:84
  115.4 2.7 %fusion.72 = f32[16,1024,64]{1,2,0:T(8,128)} fusion(bf16[16,16,1024]{2,1,0:T(8,128)(2,1)S(1)} %get-tuple-element.14, bf16[9,64,16]{1,2,0:T(8,128)(2,1)S(1)} %copy-done.16), kind=kOutput, calls=%fused_computation.97 | convolution fusion | flops 33554432 | bytes 4722688 | tf_op jit(solution)/shard_map/oc,rcw->row/dot_general | solution.py:84
  120.0 2.8 %fusion.81 = f32[16,1024,64]{1,2,0:T(8,128)} fusion(bf16[16,16,1024]{2,1,0:T(8,128)(2,1)S(1)} %get-tuple-element.9, bf16[9,64,16]{1,2,0:T(8,128)(2,1)S(1)} %copy-done.16), kind=kOutput, calls=%fused_computation.106 | convolution fusion | flops 33554432 | bytes 4722688 | tf_op jit(solution)/shard_map/oc,rcw->row/dot_general | solution.py:84
  122.7 2.7 %fusion.78 = f32[16,1024,64]{1,2,0:T(8,128)} fusion(bf16[16,16,1024]{2,1,0:T(8,128)(2,1)S(1)} %get-tuple-element.11, bf16[9,64,16]{1,2,0:T(8,128)(2,1)S(1)} %copy-done.16), kind=kOutput, calls=%fused_computation.103 | convolution fusion | flops 33554432 | bytes 4722688 | tf_op jit(solution)/shard_map/oc,rcw->row/dot_general | solution.py:84
  126.1 2.8 %fusion.75 = f32[16,1024,64]{1,2,0:T(8,128)} fusion(bf16[16,16,1024]{2,1,0:T(8,128)(2,1)S(1)} %get-tuple-element.10, bf16[9,64,16]{1,2,0:T(8,128)(2,1)S(1)} %copy-done.16), kind=kOutput, calls=%fused_computation.100 | convolution fusion | flops 33554432 | bytes 4722688 | tf_op jit(solution)/shard_map/oc,rcw->row/dot_general | solution.py:84
  131.5 2.7 %fusion.63 = f32[16,1024,64]{1,2,0:T(8,128)} fusion(bf16[16,16,1024]{2,1,0:T(8,128)(2,1)S(1)} %get-tuple-element.5, bf16[9,64,16]{1,2,0:T(8,128)(2,1)S(1)} %copy-done.16), kind=kOutput, calls=%fused_computation.88 | convolution fusion | flops 33554432 | bytes 4722688 | tf_op jit(solution)/shard_map/oc,rcw->row/dot_general | solution.py:84
  134.9 2.7 %fusion.60 = f32[16,1024,64]{1,2,0:T(8,128)} fusion(bf16[16,16,1024]{2,1,0:T(8,128)(2,1)S(1)} %get-tuple-element.4, bf16[9,64,16]{1,2,0:T(8,128)(2,1)S(1)} %copy-done.16), kind=kOutput, calls=%fused_computation.85 | convolution fusion | flops 33554432 | bytes 4722688 | tf_op jit(solution)/shard_map/oc,rcw->row/dot_general | solution.py:84
  138.9 42.8 %psum.7 = f32[9,64,16]{1,2,0:T(8,128)S(1)} all-reduce(f32[9,64,16]{1,2,0:T(8,128)S(1)} %fusion.39), channel_id=1, replica_groups=mesh['lat'=4,'lon'=8] {'lat','lon'}, use_global_device_ids=true, to_apply=%region_1.2 | all-reduce | flops 9216 | bytes 73728 | tf_op jit(solution)/shard_map/psum | solution.py:99
  182.4 14.4 %fusion.12 = bf16[16,64,1024]{2,1,0:T(8,128)(2,1)} fusion(f32[16,1024,64]{1,2,0:T(8,128)} %fusion.60, f32[16,1024,64]{1,2,0:T(8,128)} %fusion.63, f32[16,1024,64]{1,2,0:T(8,128)} %fusion.66, f32[16,1024,64]{1,2,0:T(8,128)} %fusion.50, f32[16,1024,64]{1,2,0:T(8,128)} %fusion.72, f32[16,1024,64]{1,2,0:T(8,128)} %fusion.75, f32[16,1024,64]{1,2,0:T(8,128)} %fusion.81, ...), kind=kOutput, calls=%fused_computation.19 | convolution fusion | flops 42991616 | bytes 36179968 | tf_op jit(solution)/shard_map/oc,rcw->row/dot_general | solution.py:84
  201.0 1.7 fusion.34
  202.8 2.4 %fusion.38 = bf16[16,16,1024]{2,1,0:T(8,128)(2,1)} fusion(f32[16,1024,16]{1,2,0:T(8,128)S(1)} %fusion.13, f32[16,1024,16]{1,2,0:T(8,128)S(1)} %fusion.7, f32[16,1024,16]{1,2,0:T(8,128)S(1)} %fusion.10, f32[16,1024,16]{1,2,0:T(8,128)S(1)} %fusion.34, bf16[16,80,1024]{2,1,0:T(8,128)(2,1)S(1)} %copy-done.7, bf16[16,80,4]{2,1,0:T(8,128)(2,1)S(1)} %copy-done.13, ...), kind=kOutput, calls=%fused_computation.42 | convolution fusion | flops 39059456 | bytes 7354368 | tf_op jit(solution)/shard_map/oc,row->rcw/dot_general | solution.py:92
  (75 shorter events, 27.4 us)
Async XLA Ops:
  0.6 13.7 %copy-start = (bf16[1,32,6,16,128]{4,3,2,1,0:T(8,128)(2,1)S(1)}, bf16[1,32,6,16,128]{4,3,2,1,0:T(8,128)(2,1)}, u32[]{:S(2)}) copy-start(bf16[1,32,6,16,128]{4,3,2,1,0:T(8,128)(2,1)} %param.8) | copy-start | bytes 2359300
  2.1 17.6 %all-to-all-start = ((s32[32,1,6]{2,1,0:T(1,128)}), s32[32,1,6]{2,1,0:T(1,128)S(1)}, u32[]{:S(2)}, u32[]{:S(2)}) async-start(s32[32,1,6]{2,1,0:T(1,128)} %copy.29), calls=%async_computation | async-start | bytes 32768 | tf_op jit(solution)/shard_map/all_to_all | solution.py:33
  14.3 11.4 %copy-start.2 = (bf16[16,64,1024]{2,1,0:T(8,128)(2,1)S(1)}, bf16[16,64,1024]{2,1,0:T(8,128)(2,1)}, u32[]{:S(2)}) copy-start(bf16[16,64,1024]{2,1,0:T(8,128)(2,1)} %param.13) | copy-start | bytes 6291460
  19.7 33.5 %all-to-all-start.1 = ((bf16[32,6,2048]{2,1,0:T(8,128)(2,1)}), bf16[32,6,2048]{2,1,0:T(8,128)(2,1)}, u32[]{:S(2)}, u32[]{:S(2)}) async-start(bf16[32,6,2048]{2,1,0:T(8,128)(2,1)} %reshape.119), calls=%async_computation.1 | async-start | bytes 2097152 | tf_op jit(solution)/shard_map/all_to_all | solution.py:32
  82.4 2.5 %copy-start.16 = (bf16[9,64,16]{1,2,0:T(8,128)(2,1)S(1)}, bf16[9,64,16]{1,2,0:T(8,128)(2,1)}, u32[]{:S(2)}) copy-start(bf16[9,64,16]{1,2,0:T(8,128)(2,1)} %param.12) | copy-start | bytes 55300
  82.6 5.0 %copy-start.5 = (bf16[16,80,1024]{2,1,0:T(8,128)(2,1)}, bf16[16,80,1024]{2,1,0:T(8,128)(2,1)S(1)}, u32[]{:S(2)}) copy-start(bf16[16,80,1024]{2,1,0:T(8,128)(2,1)S(1)} %constant_dynamic-update-slice_fusion) | copy-start | bytes 7864324
  82.8 16.4 %collective-permute-start.1 = (bf16[16,80,4]{2,1,0:T(8,128)(2,1)S(1)}, bf16[16,80,4]{2,1,0:T(8,128)(2,1)S(1)}, u32[]{:S(2)}, u32[]{:S(2)}) collective-permute-start(bf16[16,80,4]{2,1,0:T(8,128)(2,1)S(1)} %get-tuple-element.16), channel_id=1, source_target_pairs={{1,0},{2,1},{3,2},{4,3},{5,4},{6,5},{7,6},{0,7},{9,8},{10,9},{11,1... | collective-permute-start | bytes 30728 | tf_op jit(solution)/shard_map/ppermute | solution.py:21
  84.3 14.9 %collective-permute-start = (bf16[16,80,4]{2,1,0:T(8,128)(2,1)S(1)}, bf16[16,80,4]{2,1,0:T(8,128)(2,1)S(1)}, u32[]{:S(2)}, u32[]{:S(2)}) collective-permute-start(bf16[16,80,4]{2,1,0:T(8,128)(2,1)S(1)} %get-tuple-element.17), channel_id=1, source_target_pairs={{0,1},{1,2},{2,3},{3,4},{4,5},{5,6},{6,7},{7,0},{8,9},{9,10},{10,1... | collective-permute-start | bytes 30728 | tf_op jit(solution)/shard_map/ppermute | solution.py:18
  99.2 13.0 %copy-start.12 = (bf16[16,80,4]{2,1,0:T(8,128)(2,1)}, bf16[16,80,4]{2,1,0:T(8,128)(2,1)S(1)}, u32[]{:S(2)}) copy-start(bf16[16,80,4]{2,1,0:T(8,128)(2,1)S(1)} %collective-permute-done) | copy-start | bytes 30724
  106.0 4.4 %copy-start.6 = (bf16[16,80,1024]{2,1,0:T(8,128)(2,1)S(1)}, bf16[16,80,1024]{2,1,0:T(8,128)(2,1)}, u32[]{:S(2)}) copy-start(bf16[16,80,1024]{2,1,0:T(8,128)(2,1)} %copy-done.5) | copy-start | bytes 7864324
  107.6 10.6 %collective-permute-start.2 = (bf16[4,80,1032]{2,1,0:T(8,128)(2,1)S(1)}, bf16[4,80,1032]{2,1,0:T(8,128)(2,1)S(1)}, u32[]{:S(2)}, u32[]{:S(2)}) collective-permute-start(bf16[4,80,1032]{2,1,0:T(8,128)(2,1)S(1)} %get-tuple-element.12), channel_id=1, source_target_pairs={{0,8},{8,16},{16,24},{1,9},{9,17},{17,25},{2,10},{10,18},{18,26},{... | collective-permute-start | bytes 1981448 | tf_op jit(solution)/shard_map/ppermute | solution.py:18
  108.9 9.3 %collective-permute-start.3 = (bf16[4,80,1032]{2,1,0:T(8,128)(2,1)S(1)}, bf16[4,80,1032]{2,1,0:T(8,128)(2,1)S(1)}, u32[]{:S(2)}, u32[]{:S(2)}) collective-permute-start(bf16[4,80,1032]{2,1,0:T(8,128)(2,1)S(1)} %get-tuple-element.13), channel_id=1, source_target_pairs={{8,0},{16,8},{24,16},{9,1},{17,9},{25,17},{10,2},{18,10},{26,18},{... | collective-permute-start | bytes 1981448 | tf_op jit(solution)/shard_map/ppermute | solution.py:21
  115.4 2.8 %copy-start.3 = (bf16[16,80,1032]{2,1,0:T(8,128)(2,1)S(1)}, bf16[16,80,1032]{2,1,0:T(8,128)(2,1)}, u32[]{:S(2)}) copy-start(bf16[16,80,1032]{2,1,0:T(8,128)(2,1)} %concatenate.32) | copy-start | bytes 7925764
  118.2 0.9 copy-start.14
  118.2 1.1 copy-start.8
  182.4 14.4 %copy-start.4 = (bf16[16,80,1032]{2,1,0:T(8,128)(2,1)S(1)}, bf16[16,80,1032]{2,1,0:T(8,128)(2,1)}, u32[]{:S(2)}) copy-start(bf16[16,80,1032]{2,1,0:T(8,128)(2,1)} %concatenate.32) | copy-start | bytes 7925764
  182.4 14.4 %copy-start.9 = (bf16[4,80,1032]{2,1,0:T(8,128)(2,1)S(1)}, bf16[4,80,1032]{2,1,0:T(8,128)(2,1)}, u32[]{:S(2)}) copy-start(bf16[4,80,1032]{2,1,0:T(8,128)(2,1)} %copy-done.8) | copy-start | bytes 1981444
  197.2 1.1 copy-start.15
  199.4 1.2 copy-start.10
  199.4 1.5 copy-start.11
  201.0 1.8 copy-start.7
  201.0 1.8 copy-start.13
  201.0 4.1 %copy-start.1 = (bf16[1,32,6,16,128]{4,3,2,1,0:T(8,128)(2,1)S(1)}, bf16[1,32,6,16,128]{4,3,2,1,0:T(8,128)(2,1)}, u32[]{:S(2)}) copy-start(bf16[1,32,6,16,128]{4,3,2,1,0:T(8,128)(2,1)} %param.8) | copy-start | bytes 2359300
where the time goes:
time: 206 us; the launch traced here: 205 us
  matrix products  56 us (27%)
  blocking collectives  42.8 us (21%)
  waiting for transfers between devices  35.8 us (17%)
  other arithmetic  29.2 us (14%)
  local copies, waits for them, and re-layouts  22.4 us (11%)
  starting transfers between devices  18.1 us (9%)
    psum x1, blocking collectives, local(): total_grad = lax.psum(local_grad, ('lat', 'lon'))  42.8 us
    dot_general x9, matrix products, local(): jnp.einsum('oc,rcw->row', conv_weight[tap_number], shifted, preferred_ele...  36.3 us
    all_to_all x1, waiting for transfers between devices, route(): lax.all_to_all(payload, ('lat', 'lon'), split_axis=0, concat_axis=0, tile...  24.2 us
    scatter-add x1, other arithmetic, local(): jax.ops.segment_sum(contributions.reshape(owners * capacity, variables, p...  23.9 us
    ppermute x2, waiting for transfers between devices, extended(): lax.ppermute(lax.slice_in_dim(block, 0, width, axis=dim), axis, backward)  11.6 us
    dot_general x9, matrix products, local(): jnp.einsum('oc,row->rcw', conv_weight[tap_number], back_piece, preferred_...  11.1 us
    all_to_all x1, starting transfers between devices, route(): lax.all_to_all(targets, ('lat', 'lon'), split_axis=0, concat_axis=0, tile...  7.3 us
    concatenate x1, local copies, waits for them, and re-layouts, extended(): block = jnp.concatenate([low, block, high], axis=dim)  6.77 us
  transfers between devices with their start and end apart: 6, of which 2 were waited for; matrix products, arithmetic and copies ran while one was open for 12% of the time, Pallas kernels for 0%

commit v1 on v0

v1 whole, which is shorter than its diff:
```python
import functools
import math

import jax
import jax.numpy as jnp
from jax import lax
from jax.experimental import pallas as pl
from jax.experimental.pallas import tpu as pltpu
from jax.sharding import PartitionSpec as P

RATE = 4
EDGE = 128
MESH = pl.DeviceIdType.MESH
F32 = jnp.float32
BF16 = jnp.bfloat16
SIDES = [(-1, -1), (-1, 0), (-1, 1), (0, -1), (0, 1), (1, -1), (1, 0), (1, 1)]


def span(step, total, width):
    before, size = width
    if step < 0:
        return (0, size), (before + total, size)
    if step > 0:
        return (total - size, size), (before - size, size)
    return (0, total), (before, total)


def halo_copies(field, padded, send, recv, nlat, nlon):
    lat, lon = lax.axis_index("lat"), lax.axis_index("lon")
    rows, _, cols = field.shape
    made = []
    for k, (dr, dc) in enumerate(SIDES):
        (r0, rn), (pr, _) = span(dr, rows, (RATE, RATE))
        (c0, cn), (pc, _) = span(dc, cols, (EDGE, EDGE))
        to_lat, from_lat = lat + dr, lat - dr
        copy = pltpu.make_async_remote_copy(
            src_ref=field.at[pl.ds(r0, rn), :, pl.ds(c0, cn)],
            dst_ref=padded.at[pl.ds(pr, rn), :, pl.ds(pc, cn)],
            send_sem=send.at[k],
            recv_sem=recv.at[k],
            device_id=(lax.rem(to_lat + nlat, nlat), lax.rem(lon + dc + nlon, nlon)),
            device_id_type=MESH,
        )
        sends = (to_lat >= 0) & (to_lat < nlat)
        gets = (from_lat >= 0) & (from_lat < nlat)
        made.append((dr, sends, gets, copy))
    return made


def halo_do(made, what):
    for dr, sends, gets, copy in made:
        cond = gets if what == "wait_recv" else sends
        act = getattr(copy, what)
        if dr == 0:
            act()
        else:
            pl.when(cond)(act)


def zero_border(padded, rows, nlat):
    lat = lax.axis_index("lat")

    @pl.when(lat == 0)
    def _():
        padded[0:RATE] = jnp.zeros((RATE,) + padded.shape[1:], padded.dtype)

    @pl.when(lat == nlat - 1)
    def _():
        padded[RATE + rows : 2 * RATE + rows] = jnp.zeros(
            (RATE,) + padded.shape[1:], padded.dtype
        )


def exchange_kernel(
    nlat, nlon, pay, tgt, g, wb, arr, tarr, ig, gp, psend, precv, tsend, trecv, hsend, hrecv, lsem
):
    lat, lon = lax.axis_index("lat"), lax.axis_index("lon")
    n = nlat * nlon
    me = lat * nlon + lon
    rows, _, cols = g.shape
    nvars = ig.shape[1]
    zero_border(gp, rows, nlat)
    own_g = pltpu.make_async_copy(
        g, gp.at[pl.ds(RATE, rows), :, pl.ds(EDGE, cols)], lsem.at[0]
    )
    own_g.start()
    own_p = pltpu.make_async_copy(pay.at[me], arr.at[me], lsem.at[1])
    own_t = pltpu.make_async_copy(tgt.at[me], tarr.at[me], lsem.at[2])
    own_p.start()
    own_t.start()

    barrier = pltpu.get_barrier_semaphore()

    def greet(i, carry):
        peer = lax.rem(me + i, n)
        pl.semaphore_signal(
            barrier, inc=1, device_id=(peer // nlon, lax.rem(peer, nlon)), device_id_type=MESH
        )
        return carry

    lax.fori_loop(1, n, greet, 0)
    pl.semaphore_wait(barrier, n - 1)

    def block(i, forward):
        peer = lax.rem(me + i, n) if forward else lax.rem(me + n - i, n)
        slot = me if forward else peer
        where = (peer // nlon, lax.rem(peer, nlon))
        return (
            pltpu.make_async_remote_copy(
                pay.at[peer], arr.at[slot], psend.at[i], precv.at[slot],
                device_id=where, device_id_type=MESH,
            ),
            pltpu.make_async_remote_copy(
                tgt.at[peer], tarr.at[slot], tsend.at[i], trecv.at[slot],
                device_id=where, device_id_type=MESH,
            ),
        )

    halo = halo_copies(g, gp, hsend, hrecv, nlat, nlon)

    def send(i, carry):
        data, number = block(i, True)
        number.start()
        data.start()
        return carry

    lax.fori_loop(1, n, send, 0)
    halo_do(halo, "start")
    own_g.wait()
    halo_do(halo, "wait_recv")

    def back(r, carry):
        stack = jnp.concatenate([gp[r + 2 * RATE], gp[r + RATE], gp[r]], axis=0)
        y = jnp.dot(wb[...], stack, preferred_element_type=F32)
        width = cols + 2 * EDGE
        low = pltpu.roll(y[0:nvars], width - RATE, 1)
        high = pltpu.roll(y[2 * nvars : 3 * nvars], RATE, 1)
        total = low + y[nvars : 2 * nvars] + high
        ig[r] = total[:, EDGE : EDGE + cols].astype(BF16)
        return carry

    lax.fori_loop(0, rows, back, 0)
    halo_do(halo, "wait_send")
    own_p.wait()
    own_t.wait()

    def finish(i, carry):
        data, number = block(i, False)
        number.wait_recv()
        data.wait_recv()
        number.wait_send()
        data.wait_send()
        return carry

    lax.fori_loop(1, n, finish, 0)


def scatter_kernel(cap, tgt, arr, x, acc):
    n = arr.shape[0]
    rows, nvars, cols = x.shape
    across = cols // EDGE
    acc[...] = jnp.zeros_like(acc)

    def add(s, carry):
        for j in range(cap):
            q = tgt[s, 0, j]
            acc[q] = acc[q] + arr[s, j * nvars : (j + 1) * nvars, :].astype(F32)
        return carry

    lax.fori_loop(0, n, add, 0)

    def store(r, carry):
        for c in range(across):
            x[r, :, c * EDGE : (c + 1) * EDGE] = acc[r * across + c].astype(BF16)
        return carry

    lax.fori_loop(0, rows, store, 0)


def conv_kernel(
    nlat, nlon, scale, x, g, wf, feat, dw,
    xp, xs, gv, acc, latbuf, part, lonbuf, done,
    hsend, hrecv, asend, arecv, bsend, brecv, csend, crecv, lsem,
):
    lat, lon = lax.axis_index("lat"), lax.axis_index("lon")
    rows, nvars, cols = x.shape
    outs = g.shape[1]
    chunk = outs // nlat
    width = cols + 2 * EDGE
    zero_border(xp, rows, nlat)
    own_g = pltpu.make_async_copy(g, gv, lsem.at[0])
    own_x = pltpu.make_async_copy(
        x, xp.at[pl.ds(RATE, rows), :, pl.ds(EDGE, cols)], lsem.at[1]
    )
    own_x.start()
    own_g.start()
    barrier = pltpu.get_barrier_semaphore()

    def hello(peer_lat, peer_lon):
        pl.semaphore_signal(barrier, inc=1, device_id=(peer_lat, peer_lon), device_id_type=MESH)

    def greet_lat(i, carry):
        hello(lax.rem(lat + i, nlat), lon)
        return carry

    def greet_lon(i, carry):
        hello(lat, lax.rem(lon + i, nlon))
        return carry

    lax.fori_loop(1, nlat, greet_lat, 0)
    lax.fori_loop(1, nlon, greet_lon, 0)
    for dr, dc in SIDES:
        if dr != 0 and dc != 0:
            ok = (lat + dr >= 0) & (lat + dr < nlat)
            pl.when(ok)(
                functools.partial(
                    hello, lax.rem(lat + dr + nlat, nlat), lax.rem(lon + dc + nlon, nlon)
                )
            )
    corners = 2 * (lat > 0).astype(jnp.int32) + 2 * (lat < nlat - 1).astype(jnp.int32)
    pl.semaphore_wait(barrier, nlat - 1 + nlon - 1 + corners)

    halo = halo_copies(x, xp, hsend, hrecv, nlat, nlon)
    halo_do(halo, "start")
    own_x.wait()
    own_g.wait()
    halo_do(halo, "wait_recv")

    def shift(r, carry):
        row = xp[r].astype(F32)
        xs[0, r] = pltpu.roll(row, RATE, 1)[:, EDGE : EDGE + cols].astype(BF16)
        xs[1, r] = row[:, EDGE : EDGE + cols].astype(BF16)
        xs[2, r] = pltpu.roll(row, width - RATE, 1)[:, EDGE : EDGE + cols].astype(BF16)
        return carry

    lax.fori_loop(0, rows + 2 * RATE, shift, 0)

    def taps(r):
        return jnp.concatenate(
            [xs[b, r + a * RATE] for a in range(3) for b in range(3)], axis=0
        )

    acc[...] = jnp.zeros_like(acc)

    def grad(r, carry):
        acc[...] += lax.dot_general(
            gv[r], taps(r), (((1,), (1,)), ((), ())), preferred_element_type=F32
        )
        return carry

    lax.fori_loop(0, rows, grad, 0)

    def forward(r, carry):
        feat[r] = jnp.dot(wf[...], taps(r), preferred_element_type=F32).astype(BF16)
        return carry

    def rows_of(which):
        return pl.ds(pl.multiple_of(which * chunk, chunk), chunk)

    def scatter(i, out):
        peer = lax.rem(lat + i, nlat) if out else lax.rem(lat + nlat - i, nlat)
        slot = lat if out else peer
        return pltpu.make_async_remote_copy(
            acc.at[rows_of(peer)], latbuf.at[slot], asend.at[i], arecv.at[slot],
            device_id=(peer, lon), device_id_type=MESH,
        )

    def swap(i, out):
        peer = lax.rem(lon + i, nlon) if out else lax.rem(lon + nlon - i, nlon)
        slot = lon if out else peer
        return pltpu.make_async_remote_copy(
            part, lonbuf.at[slot], bsend.at[i], brecv.at[slot],
            device_id=(lat, peer), device_id_type=MESH,
        )

    def collect(i, out):
        peer = lax.rem(lat + i, nlat) if out else lax.rem(lat + nlat - i, nlat)
        mine = lat if out else peer
        return pltpu.make_async_remote_copy(
            done.at[mine], done.at[mine], csend.at[i], crecv.at[mine],
            device_id=(peer, lon), device_id_type=MESH,
        )

    for i in range(1, nlat):
        scatter(i, True).start()
    latbuf[lat] = acc[rows_of(lat)]
    half = rows // 2
    lax.fori_loop(0, half, forward, 0)
    for i in range(1, nlat):
        scatter(i, False).wait_recv()
    part[...] = jnp.sum(latbuf[...], axis=0)
    for i in range(1, nlon):
        swap(i, True).start()
    lonbuf[lon] = part[...]
    lax.fori_loop(half, rows, forward, 0)
    for i in range(1, nlon):
        swap(i, False).wait_recv()
    done[lat] = jnp.sum(lonbuf[...], axis=0) * scale
    for i in range(1, nlat):
        collect(i, True).start()
    for i in range(1, nlat):
        scatter(i, True).wait_send()
    for i in range(1, nlon):
        swap(i, True).wait_send()
    halo_do(halo, "wait_send")
    for i in range(1, nlat):
        collect(i, False).wait_recv()
    dw[...] = done[...]
    for i in range(1, nlat):
        collect(i, True).wait_send()


VM = pl.BlockSpec(memory_space=pltpu.VMEM)
ANY = pl.BlockSpec(memory_space=pl.ANY)


def dmas(*counts):
    return [pltpu.SemaphoreType.DMA((count,)) for count in counts]


def local(
    source_elements, remap_weights, element_index, patch_index, block_counts, conv_weight, cotangent
):
    nlat, nlon = lax.axis_size("lat"), lax.axis_size("lon")
    local_weights = remap_weights[0]
    chosen = element_index[0]
    targets = patch_index[0]
    counts = block_counts[0]
    owners, cap, points, cells = local_weights.shape
    _, outs, nvars = conv_weight.shape
    rows, _, cols = cotangent.shape
    patches = rows * cols // cells
    element_rows = source_elements[chosen].reshape(owners, cap, points, nvars)
    blocks = jnp.einsum(
        "dkjc,dkjp->dkcp", element_rows, local_weights, preferred_element_type=F32
    ).astype(BF16)
    payload = blocks.reshape(owners, cap * nvars, cells)
    live = jnp.arange(cap, dtype=jnp.int32)[None, :] < counts[:, None]
    numbers = jnp.where(live, targets, patches)
    numbers = jnp.pad(numbers, ((0, 0), (0, 128 - cap)))[:, None, :]
    taps = conv_weight.reshape(3, 3, outs, nvars)
    wb = taps.transpose(1, 3, 0, 2).reshape(3 * nvars, 3 * outs)
    wf = taps.transpose(2, 0, 1, 3).reshape(outs, 9 * nvars)
    width = cols + 2 * EDGE
    arrived, arrived_numbers, input_grad = pl.pallas_call(
        functools.partial(exchange_kernel, nlat, nlon),
        out_shape=(
            jax.ShapeDtypeStruct(payload.shape, BF16),
            jax.ShapeDtypeStruct(numbers.shape, jnp.int32),
            jax.ShapeDtypeStruct((rows, nvars, cols), BF16),
        ),
        in_specs=[ANY, ANY, ANY, VM],
        out_specs=(ANY, ANY, VM),
        scratch_shapes=[pltpu.VMEM((rows + 2 * RATE, outs, width), BF16)]
        + dmas(owners, owners, owners, owners, 8, 8, 3),
        compiler_params=pltpu.CompilerParams(
            collective_id=0, has_side_effects=True, vmem_limit_bytes=32 << 20
        ),
    )(payload, numbers, cotangent, wb)
    remapped = pl.pallas_call(
        functools.partial(scatter_kernel, cap),
        out_shape=jax.ShapeDtypeStruct((rows, nvars, cols), BF16),
        in_specs=[pl.BlockSpec(memory_space=pltpu.SMEM), VM],
        out_specs=VM,
        scratch_shapes=[pltpu.VMEM((patches + 1, nvars, cells), F32)],
        compiler_params=pltpu.CompilerParams(vmem_limit_bytes=32 << 20),
    )(arrived_numbers, arrived)
    chunk = outs // nlat
    scale = 1.0 / math.sqrt(rows * cols * nlat * nlon)
    features, grads = pl.pallas_call(
        functools.partial(conv_kernel, nlat, nlon, scale),
        out_shape=(
            jax.ShapeDtypeStruct((rows, outs, cols), BF16),
            jax.ShapeDtypeStruct((nlat, chunk, 9 * nvars), F32),
        ),
        in_specs=[ANY, ANY, VM],
        out_specs=(VM, VM),
        scratch_shapes=[
            pltpu.VMEM((rows + 2 * RATE, nvars, width), BF16),
            pltpu.VMEM((3, rows + 2 * RATE, nvars, cols), BF16),
            pltpu.VMEM((rows, outs, cols), BF16),
            pltpu.VMEM((outs, 9 * nvars), F32),
            pltpu.VMEM((nlat, chunk, 9 * nvars), F32),
            pltpu.VMEM((chunk, 9 * nvars), F32),
            pltpu.VMEM((nlon, chunk, 9 * nvars), F32),
            pltpu.VMEM((nlat, chunk, 9 * nvars), F32),
        ]
        + dmas(8, 8, nlat, nlat, nlon, nlon, nlat, nlat, 2),
        compiler_params=pltpu.CompilerParams(
            collective_id=1, has_side_effects=True, vmem_limit_bytes=40 << 20
        ),
    )(remapped, cotangent, wf)
    weight_grad = grads.reshape(outs, 9, nvars).transpose(1, 0, 2)
    return features, input_grad, weight_grad


def solution(mesh):
    in_specs = (
        P(("lat", "lon"), None),
        P(("lat", "lon"), None, None, None, None),
        P(("lat", "lon"), None, None),
        P(("lat", "lon"), None, None),
        P(("lat", "lon"), None),
        P(),
        P("lat", None, "lon"),
    )
    out_specs = (P("lat", None, "lon"), P("lat", None, "lon"), P())
    return jax.shard_map(local, mesh=mesh, in_specs=in_specs, out_specs=out_specs, check_vma=False)
```

time: 206 us -> 82 us (0.40)
  Pallas kernels: 0 us -> 65.5 us
  matrix products: 56 us -> 1.56 us
  blocking collectives: 42.8 us -> 0 us
  waiting for transfers between devices: 35.8 us -> 0 us
  other arithmetic: 29.2 us -> 1.49 us
  starting transfers between devices: 18.1 us -> 0 us
  local copies, waits for them, and re-layouts: 22.4 us -> 12.4 us
    pallas_call x0 -> x3, Pallas kernels: none -> 65.5 us  [the longest x1 37.1 us: local(): pl.pallas_call(functools.partial(exchange_kernel, nlat, nlon), out_shape=...]
    dot_general x27 -> x0, matrix products: 53.2 us -> none  [the longest x9 36.3 us: local(): jnp.einsum('oc,rcw->row', conv_weight[tap_number], shifted, preferred_ele...]
    psum x1 -> x0, blocking collectives: 42.8 us -> none  [local(): total_grad = lax.psum(local_grad, ('lat', 'lon'))]
    all_to_all x2 -> x0, waiting for transfers between devices: 24.2 us -> none  [the longest x1 24.2 us: route(): lax.all_to_all(payload, ('lat', 'lon'), split_axis=0, concat_axis=0, tile...]
    scatter-add x1 -> x0, other arithmetic: 23.9 us -> none  [local(): jax.ops.segment_sum(contributions.reshape(owners * capacity, variables, p...]
    all_to_all x2 -> x0, starting transfers between devices: 13.3 us -> none  [the longest x1 7.3 us: route(): lax.all_to_all(targets, ('lat', 'lon'), split_axis=0, concat_axis=0, tile...]
    ppermute x4 -> x0, waiting for transfers between devices: 11.6 us -> none  [the longest x2 11.6 us: extended(): lax.ppermute(lax.slice_in_dim(block, 0, width, axis=dim), axis, backward)]
    concatenate x2 -> x0, local copies, waits for them, and re-layouts: 6.95 us -> none  [the longest x1 6.77 us: extended(): block = jnp.concatenate([low, block, high], axis=dim)]
  transfers between devices with their start and end apart: 6 -> 0, of which waited for: 2 -> 0; matrix products, arithmetic and copies ran while one was open for 12% -> 0% of each run, Pallas kernels for 0% -> 0%
where the time goes in v1:
time: 82 us; the launch traced here: 81.6 us
  Pallas kernels  65.5 us (80%)
  local copies, waits for them, and re-layouts  12.4 us (15%)
  matrix products  1.56 us (2%)
  other arithmetic  1.49 us (2%)
    pallas_call x1, Pallas kernels, local(): pl.pallas_call(functools.partial(exchange_kernel, nlat, nlon), out_shape=...  37.1 us
    pallas_call x1, Pallas kernels, local(): pl.pallas_call(functools.partial(conv_kernel, nlat, nlon, scale), out_sha...  26.7 us
    unnamed x9, local copies, waits for them, and re-layouts  6.04 us
    gather x1, local copies, waits for them, and re-layouts, local(): element_rows = source_elements[chosen].reshape(owners, cap, points, nvars)  2 us
    pallas_call x1, Pallas kernels, local(): pl.pallas_call(functools.partial(scatter_kernel, cap), out_shape=jax.Shap...  1.7 us

profile of v1, /device:TPU:0, one launch (start us, length us, event | category | flops | bytes accessed | tf_op | source)
XLA Modules:
  0.0 81.6 jit_solution(4214666292225670992)
XLA Ops:
  0.6 0.0 copy-start
  0.6 0.8 compare_select_fusion
  1.4 0.1 copy.15
  1.5 0.1 reshape.61
  1.6 0.8 copy.17
  2.4 0.7 bitcast_select_fusion
  3.1 0.8 %copy.19.wf = bf16[64,144]{1,0:T(8,128)(2,1)S(1)} copy(bf16[64,144]{0,1:T(8,128)(2,1)} %bitcast.25) | data formatting | bytes 36864 | tf_op jit(solution)/shard_map/reshape | solution.py:343
  4.0 0.8 copy.18
  4.8 0.1 reshape.56.wb
  4.9 0.0 copy-start.1
  4.9 2.0 %gather_fusion = bf16[192,256]{1,0:T(8,128)(2,1)S(1)} fusion(bf16[512,256]{1,0:T(8,128)(2,1)} %param.7, s32[1024]{0:T(1024)S(1)} %pad_clamp_fusion), kind=kCustom, calls=%fused_computation | custom fusion | bytes 197376 | tf_op jit(solution)/shard_map/gather | solution.py:333
  6.9 1.4 %reshape.53 = bf16[32,6,16,16]{3,2,1,0:T(8,128)(2,1)} reshape(bf16[192,256]{1,0:T(8,128)(2,1)S(1)} %gather_fusion) | data formatting | bytes 196608 | tf_op jit(solution)/shard_map/reshape | solution.py:333
  8.3 0.0 copy-done
  8.3 1.6 %convolution_convert_fusion = bf16[32,6,16,128]{3,2,1,0:T(8,128)(2,1)S(1)} fusion(bf16[32,6,16,16]{3,2,1,0:T(8,128)(2,1)} %reshape.53, bf16[1,32,6,16,128]{4,3,2,1,0:T(8,128)(2,1)S(1)} %copy-done), kind=kOutput, calls=%fused_computation.1 | convolution fusion | flops 12976128 | bytes 1671168 | tf_op jit(solution)/shard_map/dkjc,dkjp->dkcp/dot_general | solution.py:334
  9.9 0.0 copy-done.1
  9.9 37.1 %shard_map.94 = (bf16[32,96,128]{2,1,0:T(8,128)(2,1)S(1)}, s32[32,1,128]{2,1,0:T(1,128)S(1)}, bf16[16,16,1024]{2,1,0:T(8,128)(2,1)S(1)}) custom-call(bf16[32,96,128]{2,1,0:T(8,128)(2,1)S(1)} %bitcast.23, s32[32,1,128]{2,1,0:T(1,128)S(1)} %bitcast.24, bf16[16,64,1024]{2,1,0:T(8,128)(2,1)S(1)} %copy-done.1, bf16[48,192]{1,0:T(8,128)(2,1)S(1)} %reshape.56.wb), custom_call_target="tpu_custom_call" | custom-call | tf_op jit(solution)/shard_map/pallas_call | solution.py:345
  47.0 1.7 %shard_map.95.x = bf16[16,16,1024]{2,1,0:T(8,128)(2,1)S(1)} custom-call(s32[32,1,128]{2,1,0:T(1,128)S(1)} %get-tuple-element.8.tgt, bf16[32,96,128]{2,1,0:T(8,128)(2,1)S(1)} %get-tuple-element.9.arr), custom_call_target="tpu_custom_call" | custom-call | tf_op jit(solution)/shard_map/pallas_call | solution.py:360
  48.7 26.7 %shard_map.96 = (bf16[16,64,1024]{2,1,0:T(8,128)(2,1)S(1)}, f32[4,16,144]{2,1,0:T(8,128)S(1)}) custom-call(bf16[16,16,1024]{2,1,0:T(8,128)(2,1)S(1)} %shard_map.95.x, bf16[16,64,1024]{2,1,0:T(8,128)(2,1)S(1)} %copy-done.1, bf16[64,144]{1,0:T(8,128)(2,1)S(1)} %copy.19.wf), custom_call_target="tpu_custom_call" | custom-call | tf_op jit(solution)/shard_map/pallas_call | solution.py:370
  75.4 0.0 copy-start.2
  75.4 1.3 %copy-done.2 = bf16[16,64,1024]{2,1,0:T(8,128)(2,1)} copy-done((bf16[16,64,1024]{2,1,0:T(8,128)(2,1)}, bf16[16,64,1024]{2,1,0:T(8,128)(2,1)S(1)}, u32[]{:S(2)}) %copy-start.2) | copy-done | bytes 2097176
  76.7 0.2 copy.20
  76.9 0.8 reshape.58
  77.7 3.1 %copy.24 = bf16[16,64,1024]{2,1,0:T(8,128)(2,1)} copy(bf16[16,64,1024]{2,1,0:T(8,128)(2,1)} %copy-done.2) | data formatting | bytes 4194304
  80.8 0.8 copy.25
  (2 shorter events, 0.0 us)
Async XLA Ops:
  0.6 7.7 %copy-start = (bf16[1,32,6,16,128]{4,3,2,1,0:T(8,128)(2,1)S(1)}, bf16[1,32,6,16,128]{4,3,2,1,0:T(8,128)(2,1)}, u32[]{:S(2)}) copy-start(bf16[1,32,6,16,128]{4,3,2,1,0:T(8,128)(2,1)} %param.8) | copy-start | bytes 2359300
  4.9 5.0 %copy-start.1 = (bf16[16,64,1024]{2,1,0:T(8,128)(2,1)S(1)}, bf16[16,64,1024]{2,1,0:T(8,128)(2,1)}, u32[]{:S(2)}) copy-start(bf16[16,64,1024]{2,1,0:T(8,128)(2,1)} %g.3) | copy-start | bytes 6291460
  75.4 1.3 %copy-start.2 = (bf16[16,64,1024]{2,1,0:T(8,128)(2,1)}, bf16[16,64,1024]{2,1,0:T(8,128)(2,1)S(1)}, u32[]{:S(2)}) copy-start(bf16[16,64,1024]{2,1,0:T(8,128)(2,1)S(1)} %get-tuple-element.16) | copy-start | bytes 6291460

commit v2 on v1

--- a/solution.py
+++ b/solution.py
@@ -71,8 +71,67 @@
         )
 
 
+def edge_copies(packed, landed, send, recv, nlat, nlon):
+    lat, lon = lax.axis_index("lat"), lax.axis_index("lon")
+    made = []
+    for k, (dr, dc) in enumerate(SIDES):
+        if dc == 0:
+            continue
+        to_lat, from_lat = lat + dr, lat - dr
+        copy = pltpu.make_async_remote_copy(
+            src_ref=packed.at[0 if dc < 0 else 1],
+            dst_ref=landed.at[k],
+            send_sem=send.at[k],
+            recv_sem=recv.at[k],
+            device_id=(lax.rem(to_lat + nlat, nlat), lax.rem(lon + dc + nlon, nlon)),
+            device_id_type=MESH,
+        )
+        sends = (to_lat >= 0) & (to_lat < nlat)
+        gets = (from_lat >= 0) & (from_lat < nlat)
+        made.append((dr, sends, gets, copy))
+    return made
+
+
+def pack_edges(padded, packed, rows, cols):
+    lane = lax.broadcasted_iota(jnp.int32, packed.shape[1:], 1)
+    first = jnp.zeros(packed.shape[1:], F32)
+    last = first
+    for i in range(rows):
+        here = (lane >= i * RATE) & (lane < (i + 1) * RATE)
+        head = padded[RATE + i, :, EDGE : 2 * EDGE].astype(F32)
+        tail = padded[RATE + i, :, cols : cols + EDGE].astype(F32)
+        first = jnp.where(here, pltpu.roll(head, i * RATE, 1) if i else head, first)
+        last = jnp.where(here, pltpu.roll(tail, (i + 1) * RATE, 1), last)
+    packed[0] = first.astype(BF16)
+    packed[1] = last.astype(BF16)
+
+
+def unpack_edges(landed, padded, rows, cols, nlat):
+    lat = lax.axis_index("lat")
+    for k, (dr, dc) in enumerate(SIDES):
+        if dc == 0:
+            continue
+
+        def place(k=k, dr=dr, dc=dc):
+            block = landed[k].astype(F32)
+            base = {-1: RATE + rows, 0: RATE, 1: RATE - rows}[dr]
+            taken = {-1: range(RATE), 0: range(rows), 1: range(rows - RATE, rows)}[dr]
+            for i in taken:
+                move = (EDGE - i * RATE - (0 if dc < 0 else RATE)) % EDGE
+                tile = (pltpu.roll(block, move, 1) if move else block).astype(BF16)
+                if dc < 0:
+                    padded[base + i, :, EDGE + cols : 2 * EDGE + cols] = tile
+                else:
+                    padded[base + i, :, 0:EDGE] = tile
+
+        if dr == 0:
+            place()
+        else:
+            pl.when((lat - dr >= 0) & (lat - dr < nlat))(place)
+
+
 def exchange_kernel(
-    nlat, nlon, pay, tgt, g, wb, arr, tarr, ig, gp, psend, precv, tsend, trecv, hsend, hrecv, lsem
+    nlat, nlon, pay, tgt, g, wb, arr, tarr, ig, gp, packed, landed, psend, precv, tsend, trecv, hsend, hrecv, lsem
 ):
     lat, lon = lax.axis_index("lat"), lax.axis_index("lon")
     n = nlat * nlon
@@ -99,6 +158,8 @@
         return carry
 
     lax.fori_loop(1, n, greet, 0)
+    own_g.wait()
+    pack_edges(gp, packed, rows, cols)
     pl.semaphore_wait(barrier, n - 1)
 
     def block(i, forward):
@@ -116,7 +177,11 @@
             ),
         )
 
-    halo = halo_copies(g, gp, hsend, hrecv, nlat, nlon)
+    halo = [
+        side
+        for side, (_, dc) in zip(halo_copies(g, gp, hsend, hrecv, nlat, nlon), SIDES)
+        if dc == 0
+    ] + edge_copies(packed, landed, hsend, hrecv, nlat, nlon)
 
     def send(i, carry):
         data, number = block(i, True)
@@ -124,10 +189,10 @@
         data.start()
         return carry
 
+    halo_do(halo, "start")
     lax.fori_loop(1, n, send, 0)
-    halo_do(halo, "start")
-    own_g.wait()
     halo_do(halo, "wait_recv")
+    unpack_edges(landed, gp, rows, cols, nlat)
 
     def back(r, carry):
         stack = jnp.concatenate([gp[r + 2 * RATE], gp[r + RATE], gp[r]], axis=0)
@@ -351,7 +416,11 @@
         ),
         in_specs=[ANY, ANY, ANY, VM],
         out_specs=(ANY, ANY, VM),
-        scratch_shapes=[pltpu.VMEM((rows + 2 * RATE, outs, width), BF16)]
+        scratch_shapes=[
+            pltpu.VMEM((rows + 2 * RATE, outs, width), BF16),
+            pltpu.VMEM((2, outs, EDGE), BF16),
+            pltpu.VMEM((8, outs, EDGE), BF16),
+        ]
         + dmas(owners, owners, owners, owners, 8, 8, 3),
         compiler_params=pltpu.CompilerParams(
             collective_id=0, has_side_effects=True, vmem_limit_bytes=32 << 20

time: 82 us -> 71.4 us (0.87)
  Pallas kernels: 65.5 us -> 54.9 us
    pallas_call x1, Pallas kernels: 37.1 us -> 27.3 us  [local(): pl.pallas_call(functools.partial(exchange_kernel, nlat, nlon), out_shape=...]
    pallas_call x1, Pallas kernels: 26.7 us -> 25.9 us  [local(): pl.pallas_call(functools.partial(conv_kernel, nlat, nlon, scale), out_sha...]
where the time goes in v2:
time: 71.4 us; the launch traced here: 71 us
  Pallas kernels  54.9 us (77%)
  local copies, waits for them, and re-layouts  12.4 us (17%)
  matrix products  1.56 us (2%)
  other arithmetic  1.49 us (2%)
  between operations  0.72 us (1%)
    pallas_call x1, Pallas kernels, local(): pl.pallas_call(functools.partial(exchange_kernel, nlat, nlon), out_shape=...  27.3 us
    pallas_call x1, Pallas kernels, local(): pl.pallas_call(functools.partial(conv_kernel, nlat, nlon, scale), out_sha...  25.9 us
    unnamed x9, local copies, waits for them, and re-layouts  6.04 us
    gather x1, local copies, waits for them, and re-layouts, local(): element_rows = source_elements[chosen].reshape(owners, cap, points, nvars)  2 us
    pallas_call x1, Pallas kernels, local(): pl.pallas_call(functools.partial(scatter_kernel, cap), out_shape=jax.Shap...  1.68 us
    dot_general x1, matrix products, local(): jnp.einsum('dkjc,dkjp->dkcp', element_rows, local_weights, preferred_elem...  1.56 us
    reshape x1, local copies, waits for them, and re-layouts, local(): element_rows = source_elements[chosen].reshape(owners, cap, points, nvars)  1.43 us

profile of v2, /device:TPU:0, one launch (start us, length us, event | category | flops | bytes accessed | tf_op | source)
XLA Modules:
  0.0 71.0 jit_solution(7652377260644078452)
XLA Ops:
  0.6 0.0 copy-start
  0.6 0.8 %compare_select_fusion = s32[32,6,1]{0,2,1:T(1,128)S(1)} fusion(s32[1,32,6]{1,0,2:T(1,128)} %param.9), kind=kLoop, calls=%fused_computation.3 | loop fusion | flops 576 | bytes 1536 | tf_op jit(solution)/shard_map/select_n | solution.py:398
  1.4 0.1 copy.15
  1.5 0.1 reshape.61
  1.6 0.8 %copy.17 = s32[1,32,6]{2,1,0:T(8,128)S(1)} copy(s32[1,32,6]{1,0,2:T(1,128)} %param.10) | data formatting | bytes 1536 | tf_op args[3]
  2.4 0.7 %bitcast_select_fusion = s32[32,6]{1,0:T(8,128)S(1)} fusion(s32[1,32,6]{2,1,0:T(8,128)S(1)} %copy.17, s32[32]{0:T(128)} %bitcast.28), kind=kLoop, calls=%fused_computation.4 | loop fusion | flops 384 | bytes 1664 | tf_op jit(solution)/shard_map/jit(_where)/select_n | solution.py:404
  3.1 0.8 %copy.19.wf = bf16[64,144]{1,0:T(8,128)(2,1)S(1)} copy(bf16[64,144]{0,1:T(8,128)(2,1)} %bitcast.25) | data formatting | bytes 36864 | tf_op jit(solution)/shard_map/reshape | solution.py:408
  4.0 0.8 %copy.18 = bf16[3,16,3,64]{3,2,1,0:T(4,128)(2,1)S(1)} copy(bf16[3,16,3,64]{3,1,0,2:T(8,128)(2,1)} %bitcast.26) | data formatting | bytes 36864 | tf_op jit(solution)/shard_map/transpose | solution.py:407
  4.8 0.1 reshape.56.wb
  4.9 0.0 copy-start.1
  4.9 2.0 %gather_fusion = bf16[192,256]{1,0:T(8,128)(2,1)S(1)} fusion(bf16[512,256]{1,0:T(8,128)(2,1)} %param.7, s32[1024]{0:T(1024)S(1)} %pad_clamp_fusion), kind=kCustom, calls=%fused_computation | custom fusion | bytes 197376 | tf_op jit(solution)/shard_map/gather | solution.py:398
  6.9 1.4 %reshape.53 = bf16[32,6,16,16]{3,2,1,0:T(8,128)(2,1)} reshape(bf16[192,256]{1,0:T(8,128)(2,1)S(1)} %gather_fusion) | data formatting | bytes 196608 | tf_op jit(solution)/shard_map/reshape | solution.py:398
  8.3 0.0 copy-done
  8.3 1.6 %convolution_convert_fusion = bf16[32,6,16,128]{3,2,1,0:T(8,128)(2,1)S(1)} fusion(bf16[32,6,16,16]{3,2,1,0:T(8,128)(2,1)} %reshape.53, bf16[1,32,6,16,128]{4,3,2,1,0:T(8,128)(2,1)S(1)} %copy-done), kind=kOutput, calls=%fused_computation.1 | convolution fusion | flops 12976128 | bytes 1671168 | tf_op jit(solution)/shard_map/dkjc,dkjp->dkcp/dot_general | solution.py:399
  9.9 0.0 copy-done.1
  9.9 27.3 %shard_map.94 = (bf16[32,96,128]{2,1,0:T(8,128)(2,1)S(1)}, s32[32,1,128]{2,1,0:T(1,128)S(1)}, bf16[16,16,1024]{2,1,0:T(8,128)(2,1)S(1)}) custom-call(bf16[32,96,128]{2,1,0:T(8,128)(2,1)S(1)} %bitcast.23, s32[32,1,128]{2,1,0:T(1,128)S(1)} %bitcast.24, bf16[16,64,1024]{2,1,0:T(8,128)(2,1)S(1)} %copy-done.1, bf16[48,192]{1,0:T(8,128)(2,1)S(1)} %reshape.56.wb), custom_call_target="tpu_custom_call" | custom-call | tf_op jit(solution)/shard_map/pallas_call | solution.py:410
  37.2 1.7 %shard_map.95.x = bf16[16,16,1024]{2,1,0:T(8,128)(2,1)S(1)} custom-call(s32[32,1,128]{2,1,0:T(1,128)S(1)} %get-tuple-element.8.tgt, bf16[32,96,128]{2,1,0:T(8,128)(2,1)S(1)} %get-tuple-element.9.arr), custom_call_target="tpu_custom_call" | custom-call | tf_op jit(solution)/shard_map/pallas_call | solution.py:429
  38.9 25.9 %shard_map.96 = (bf16[16,64,1024]{2,1,0:T(8,128)(2,1)S(1)}, f32[4,16,144]{2,1,0:T(8,128)S(1)}) custom-call(bf16[16,16,1024]{2,1,0:T(8,128)(2,1)S(1)} %shard_map.95.x, bf16[16,64,1024]{2,1,0:T(8,128)(2,1)S(1)} %copy-done.1, bf16[64,144]{1,0:T(8,128)(2,1)S(1)} %copy.19.wf), custom_call_target="tpu_custom_call" | custom-call | tf_op jit(solution)/shard_map/pallas_call | solution.py:439
  64.8 0.0 copy-start.2
  64.8 1.3 %copy-done.2 = bf16[16,64,1024]{2,1,0:T(8,128)(2,1)} copy-done((bf16[16,64,1024]{2,1,0:T(8,128)(2,1)}, bf16[16,64,1024]{2,1,0:T(8,128)(2,1)S(1)}, u32[]{:S(2)}) %copy-start.2) | copy-done | bytes 2097176
  66.1 0.2 copy.20
  66.3 0.8 %reshape.58 = f32[64,9,16]{0,2,1:T(8,128)} reshape(f32[4,16,144]{1,0,2:T(4,128)S(1)} %copy.20) | data formatting | bytes 73728 | tf_op jit(solution)/shard_map/reshape | solution.py:462
  67.1 3.1 %copy.24 = bf16[16,64,1024]{2,1,0:T(8,128)(2,1)} copy(bf16[16,64,1024]{2,1,0:T(8,128)(2,1)} %copy-done.2) | data formatting | bytes 4194304
  70.2 0.8 %copy.25 = bf16[16,16,1024]{2,1,0:T(8,128)(2,1)} copy(bf16[16,16,1024]{2,1,0:T(8,128)(2,1)S(1)} %get-tuple-element.17) | data formatting | bytes 1048576
  (2 shorter events, 0.0 us)
Async XLA Ops:
  0.6 7.7 %copy-start = (bf16[1,32,6,16,128]{4,3,2,1,0:T(8,128)(2,1)S(1)}, bf16[1,32,6,16,128]{4,3,2,1,0:T(8,128)(2,1)}, u32[]{:S(2)}) copy-start(bf16[1,32,6,16,128]{4,3,2,1,0:T(8,128)(2,1)} %param.8) | copy-start | bytes 2359300
  4.9 5.0 %copy-start.1 = (bf16[16,64,1024]{2,1,0:T(8,128)(2,1)S(1)}, bf16[16,64,1024]{2,1,0:T(8,128)(2,1)}, u32[]{:S(2)}) copy-start(bf16[16,64,1024]{2,1,0:T(8,128)(2,1)} %g.3) | copy-start | bytes 6291460
  64.8 1.3 %copy-start.2 = (bf16[16,64,1024]{2,1,0:T(8,128)(2,1)}, bf16[16,64,1024]{2,1,0:T(8,128)(2,1)S(1)}, u32[]{:S(2)}) copy-start(bf16[16,64,1024]{2,1,0:T(8,128)(2,1)S(1)} %get-tuple-element.16) | copy-start | bytes 6291460

commit v3 on v2

--- a/solution.py
+++ b/solution.py
@@ -244,7 +244,7 @@
 
 def conv_kernel(
     nlat, nlon, scale, x, g, wf, feat, dw,
-    xp, xs, gv, acc, latbuf, part, lonbuf, done,
+    xp, packed, landed, xs, gv, acc, latbuf, part, lonbuf, done,
     hsend, hrecv, asend, arecv, bsend, brecv, csend, crecv, lsem,
 ):
     lat, lon = lax.axis_index("lat"), lax.axis_index("lon")
@@ -282,14 +282,20 @@
                     hello, lax.rem(lat + dr + nlat, nlat), lax.rem(lon + dc + nlon, nlon)
                 )
             )
+    own_x.wait()
+    pack_edges(xp, packed, rows, cols)
     corners = 2 * (lat > 0).astype(jnp.int32) + 2 * (lat < nlat - 1).astype(jnp.int32)
     pl.semaphore_wait(barrier, nlat - 1 + nlon - 1 + corners)
 
-    halo = halo_copies(x, xp, hsend, hrecv, nlat, nlon)
+    halo = [
+        side
+        for side, (_, dc) in zip(halo_copies(x, xp, hsend, hrecv, nlat, nlon), SIDES)
+        if dc == 0
+    ] + edge_copies(packed, landed, hsend, hrecv, nlat, nlon)
     halo_do(halo, "start")
-    own_x.wait()
     own_g.wait()
     halo_do(halo, "wait_recv")
+    unpack_edges(landed, xp, rows, cols, nlat)
 
     def shift(r, carry):
         row = xp[r].astype(F32)
@@ -446,6 +452,8 @@
         out_specs=(VM, VM),
         scratch_shapes=[
             pltpu.VMEM((rows + 2 * RATE, nvars, width), BF16),
+            pltpu.VMEM((2, nvars, EDGE), BF16),
+            pltpu.VMEM((8, nvars, EDGE), BF16),
             pltpu.VMEM((3, rows + 2 * RATE, nvars, cols), BF16),
             pltpu.VMEM((rows, outs, cols), BF16),
             pltpu.VMEM((outs, 9 * nvars), F32),

time: 71.4 us -> 70.5 us (0.987)
  Pallas kernels: 54.9 us -> 53.9 us
    pallas_call x1, Pallas kernels: 25.9 us -> 24.9 us  [local(): pl.pallas_call(functools.partial(conv_kernel, nlat, nlon, scale), out_sha...]
where the time goes in v3:
time: 70.5 us; the launch traced here: 70.1 us
  Pallas kernels  53.9 us (76%)
  local copies, waits for them, and re-layouts  12.4 us (18%)
  matrix products  1.56 us (2%)
  other arithmetic  1.49 us (2%)
  between operations  0.72 us (1%)
    pallas_call x1, Pallas kernels, local(): pl.pallas_call(functools.partial(exchange_kernel, nlat, nlon), out_shape=...  27.3 us
    pallas_call x1, Pallas kernels, local(): pl.pallas_call(functools.partial(conv_kernel, nlat, nlon, scale), out_sha...  24.9 us
    unnamed x9, local copies, waits for them, and re-layouts  6.04 us
    gather x1, local copies, waits for them, and re-layouts, local(): element_rows = source_elements[chosen].reshape(owners, cap, points, nvars)  2 us
    pallas_call x1, Pallas kernels, local(): pl.pallas_call(functools.partial(scatter_kernel, cap), out_shape=jax.Shap...  1.67 us
    dot_general x1, matrix products, local(): jnp.einsum('dkjc,dkjp->dkcp', element_rows, local_weights, preferred_elem...  1.56 us
    reshape x1, local copies, waits for them, and re-layouts, local(): element_rows = source_elements[chosen].reshape(owners, cap, points, nvars)  1.43 us

profile of v3, /device:TPU:0, one launch (start us, length us, event | category | flops | bytes accessed | tf_op | source)
XLA Modules:
  0.0 70.1 jit_solution(3877943766174808314)
XLA Ops:
  0.6 0.0 copy-start
  0.6 0.8 %compare_select_fusion = s32[32,6,1]{0,2,1:T(1,128)S(1)} fusion(s32[1,32,6]{1,0,2:T(1,128)} %param.9), kind=kLoop, calls=%fused_computation.3 | loop fusion | flops 576 | bytes 1536 | tf_op jit(solution)/shard_map/select_n | solution.py:404
  1.4 0.1 copy.15
  1.5 0.1 reshape.61
  1.6 0.8 %copy.17 = s32[1,32,6]{2,1,0:T(8,128)S(1)} copy(s32[1,32,6]{1,0,2:T(1,128)} %param.10) | data formatting | bytes 1536 | tf_op args[3]
  2.4 0.7 %bitcast_select_fusion = s32[32,6]{1,0:T(8,128)S(1)} fusion(s32[1,32,6]{2,1,0:T(8,128)S(1)} %copy.17, s32[32]{0:T(128)} %bitcast.28), kind=kLoop, calls=%fused_computation.4 | loop fusion | flops 384 | bytes 1664 | tf_op jit(solution)/shard_map/jit(_where)/select_n | solution.py:410
  3.1 0.8 %copy.19.wf = bf16[64,144]{1,0:T(8,128)(2,1)S(1)} copy(bf16[64,144]{0,1:T(8,128)(2,1)} %bitcast.25) | data formatting | bytes 36864 | tf_op jit(solution)/shard_map/reshape | solution.py:414
  4.0 0.8 %copy.18 = bf16[3,16,3,64]{3,2,1,0:T(4,128)(2,1)S(1)} copy(bf16[3,16,3,64]{3,1,0,2:T(8,128)(2,1)} %bitcast.26) | data formatting | bytes 36864 | tf_op jit(solution)/shard_map/transpose | solution.py:413
  4.8 0.1 reshape.56.wb
  4.9 0.0 copy-start.1
  4.9 2.0 %gather_fusion = bf16[192,256]{1,0:T(8,128)(2,1)S(1)} fusion(bf16[512,256]{1,0:T(8,128)(2,1)} %param.7, s32[1024]{0:T(1024)S(1)} %pad_clamp_fusion), kind=kCustom, calls=%fused_computation | custom fusion | bytes 197376 | tf_op jit(solution)/shard_map/gather | solution.py:404
  6.9 1.4 %reshape.53 = bf16[32,6,16,16]{3,2,1,0:T(8,128)(2,1)} reshape(bf16[192,256]{1,0:T(8,128)(2,1)S(1)} %gather_fusion) | data formatting | bytes 196608 | tf_op jit(solution)/shard_map/reshape | solution.py:404
  8.3 0.0 copy-done
  8.3 1.6 %convolution_convert_fusion = bf16[32,6,16,128]{3,2,1,0:T(8,128)(2,1)S(1)} fusion(bf16[32,6,16,16]{3,2,1,0:T(8,128)(2,1)} %reshape.53, bf16[1,32,6,16,128]{4,3,2,1,0:T(8,128)(2,1)S(1)} %copy-done), kind=kOutput, calls=%fused_computation.1 | convolution fusion | flops 12976128 | bytes 1671168 | tf_op jit(solution)/shard_map/dkjc,dkjp->dkcp/dot_general | solution.py:405
  9.9 0.0 copy-done.1
  9.9 27.3 %shard_map.94 = (bf16[32,96,128]{2,1,0:T(8,128)(2,1)S(1)}, s32[32,1,128]{2,1,0:T(1,128)S(1)}, bf16[16,16,1024]{2,1,0:T(8,128)(2,1)S(1)}) custom-call(bf16[32,96,128]{2,1,0:T(8,128)(2,1)S(1)} %bitcast.23, s32[32,1,128]{2,1,0:T(1,128)S(1)} %bitcast.24, bf16[16,64,1024]{2,1,0:T(8,128)(2,1)S(1)} %copy-done.1, bf16[48,192]{1,0:T(8,128)(2,1)S(1)} %reshape.56.wb), custom_call_target="tpu_custom_call" | custom-call | tf_op jit(solution)/shard_map/pallas_call | solution.py:416
  37.2 1.7 %shard_map.95.x = bf16[16,16,1024]{2,1,0:T(8,128)(2,1)S(1)} custom-call(s32[32,1,128]{2,1,0:T(1,128)S(1)} %get-tuple-element.8.tgt, bf16[32,96,128]{2,1,0:T(8,128)(2,1)S(1)} %get-tuple-element.9.arr), custom_call_target="tpu_custom_call" | custom-call | tf_op jit(solution)/shard_map/pallas_call | solution.py:435
  38.9 24.9 %shard_map.96 = (bf16[16,64,1024]{2,1,0:T(8,128)(2,1)S(1)}, f32[4,16,144]{2,1,0:T(8,128)S(1)}) custom-call(bf16[16,16,1024]{2,1,0:T(8,128)(2,1)S(1)} %shard_map.95.x, bf16[16,64,1024]{2,1,0:T(8,128)(2,1)S(1)} %copy-done.1, bf16[64,144]{1,0:T(8,128)(2,1)S(1)} %copy.19.wf), custom_call_target="tpu_custom_call" | custom-call | tf_op jit(solution)/shard_map/pallas_call | solution.py:445
  63.8 0.0 copy-start.2
  63.9 1.3 %copy-done.2 = bf16[16,64,1024]{2,1,0:T(8,128)(2,1)} copy-done((bf16[16,64,1024]{2,1,0:T(8,128)(2,1)}, bf16[16,64,1024]{2,1,0:T(8,128)(2,1)S(1)}, u32[]{:S(2)}) %copy-start.2) | copy-done | bytes 2097176
  65.2 0.2 copy.20
  65.3 0.8 %reshape.58 = f32[64,9,16]{0,2,1:T(8,128)} reshape(f32[4,16,144]{1,0,2:T(4,128)S(1)} %copy.20) | data formatting | bytes 73728 | tf_op jit(solution)/shard_map/reshape | solution.py:470
  66.2 3.1 %copy.24 = bf16[16,64,1024]{2,1,0:T(8,128)(2,1)} copy(bf16[16,64,1024]{2,1,0:T(8,128)(2,1)} %copy-done.2) | data formatting | bytes 4194304
  69.3 0.8 %copy.25 = bf16[16,16,1024]{2,1,0:T(8,128)(2,1)} copy(bf16[16,16,1024]{2,1,0:T(8,128)(2,1)S(1)} %get-tuple-element.17) | data formatting | bytes 1048576
  (2 shorter events, 0.0 us)
Async XLA Ops:
  0.6 7.7 %copy-start = (bf16[1,32,6,16,128]{4,3,2,1,0:T(8,128)(2,1)S(1)}, bf16[1,32,6,16,128]{4,3,2,1,0:T(8,128)(2,1)}, u32[]{:S(2)}) copy-start(bf16[1,32,6,16,128]{4,3,2,1,0:T(8,128)(2,1)} %param.8) | copy-start | bytes 2359300
  4.9 5.0 %copy-start.1 = (bf16[16,64,1024]{2,1,0:T(8,128)(2,1)S(1)}, bf16[16,64,1024]{2,1,0:T(8,128)(2,1)}, u32[]{:S(2)}) copy-start(bf16[16,64,1024]{2,1,0:T(8,128)(2,1)} %g.3) | copy-start | bytes 6291460
  63.8 1.3 %copy-start.2 = (bf16[16,64,1024]{2,1,0:T(8,128)(2,1)}, bf16[16,64,1024]{2,1,0:T(8,128)(2,1)S(1)}, u32[]{:S(2)}) copy-start(bf16[16,64,1024]{2,1,0:T(8,128)(2,1)S(1)} %get-tuple-element.16) | copy-start | bytes 6291460

commit v4 on v3

--- a/solution.py
+++ b/solution.py
@@ -304,7 +304,7 @@
         xs[2, r] = pltpu.roll(row, width - RATE, 1)[:, EDGE : EDGE + cols].astype(BF16)
         return carry
 
-    lax.fori_loop(0, rows + 2 * RATE, shift, 0)
+    lax.fori_loop(0, rows + 2 * RATE, shift, 0, unroll=4)
 
     def taps(r):
         return jnp.concatenate(
@@ -319,7 +319,7 @@
         )
         return carry
 
-    lax.fori_loop(0, rows, grad, 0)
+    lax.fori_loop(0, rows, grad, 0, unroll=4)
 
     def forward(r, carry):
         feat[r] = jnp.dot(wf[...], taps(r), preferred_element_type=F32).astype(BF16)

time: 70.5 us -> 67.7 us (0.960)
  Pallas kernels: 53.9 us -> 51.1 us
    pallas_call x1, Pallas kernels: 24.9 us -> 22.1 us  [local(): pl.pallas_call(functools.partial(conv_kernel, nlat, nlon, scale), out_sha...]
where the time goes in v4:
time: 67.7 us; the launch traced here: 67.3 us
  Pallas kernels  51.1 us (75%)
  local copies, waits for them, and re-layouts  12.4 us (18%)
  matrix products  1.56 us (2%)
  other arithmetic  1.49 us (2%)
  between operations  0.72 us (1%)
    pallas_call x1, Pallas kernels, local(): pl.pallas_call(functools.partial(exchange_kernel, nlat, nlon), out_shape=...  27.3 us
    pallas_call x1, Pallas kernels, local(): pl.pallas_call(functools.partial(conv_kernel, nlat, nlon, scale), out_sha...  22.1 us
    unnamed x9, local copies, waits for them, and re-layouts  6.04 us
    gather x1, local copies, waits for them, and re-layouts, local(): element_rows = source_elements[chosen].reshape(owners, cap, points, nvars)  2 us
    pallas_call x1, Pallas kernels, local(): pl.pallas_call(functools.partial(scatter_kernel, cap), out_shape=jax.Shap...  1.68 us
    dot_general x1, matrix products, local(): jnp.einsum('dkjc,dkjp->dkcp', element_rows, local_weights, preferred_elem...  1.56 us
    reshape x1, local copies, waits for them, and re-layouts, local(): element_rows = source_elements[chosen].reshape(owners, cap, points, nvars)  1.43 us

profile of v4, /device:TPU:0, one launch (start us, length us, event | category | flops | bytes accessed | tf_op | source)
XLA Modules:
  0.0 67.3 jit_solution(636506224074952323)
XLA Ops:
  0.6 0.0 copy-start
  0.6 0.8 %compare_select_fusion = s32[32,6,1]{0,2,1:T(1,128)S(1)} fusion(s32[1,32,6]{1,0,2:T(1,128)} %param.9), kind=kLoop, calls=%fused_computation.3 | loop fusion | flops 576 | bytes 1536 | tf_op jit(solution)/shard_map/select_n | solution.py:404
  1.4 0.1 copy.15
  1.5 0.1 reshape.61
  1.6 0.8 %copy.17 = s32[1,32,6]{2,1,0:T(8,128)S(1)} copy(s32[1,32,6]{1,0,2:T(1,128)} %param.10) | data formatting | bytes 1536 | tf_op args[3]
  2.4 0.7 %bitcast_select_fusion = s32[32,6]{1,0:T(8,128)S(1)} fusion(s32[1,32,6]{2,1,0:T(8,128)S(1)} %copy.17, s32[32]{0:T(128)} %bitcast.28), kind=kLoop, calls=%fused_computation.4 | loop fusion | flops 384 | bytes 1664 | tf_op jit(solution)/shard_map/jit(_where)/select_n | solution.py:410
  3.1 0.8 %copy.19.wf = bf16[64,144]{1,0:T(8,128)(2,1)S(1)} copy(bf16[64,144]{0,1:T(8,128)(2,1)} %bitcast.25) | data formatting | bytes 36864 | tf_op jit(solution)/shard_map/reshape | solution.py:414
  4.0 0.8 %copy.18 = bf16[3,16,3,64]{3,2,1,0:T(4,128)(2,1)S(1)} copy(bf16[3,16,3,64]{3,1,0,2:T(8,128)(2,1)} %bitcast.26) | data formatting | bytes 36864 | tf_op jit(solution)/shard_map/transpose | solution.py:413
  4.8 0.1 reshape.56.wb
  4.9 0.0 copy-start.1
  4.9 2.0 %gather_fusion = bf16[192,256]{1,0:T(8,128)(2,1)S(1)} fusion(bf16[512,256]{1,0:T(8,128)(2,1)} %param.7, s32[1024]{0:T(1024)S(1)} %pad_clamp_fusion), kind=kCustom, calls=%fused_computation | custom fusion | bytes 197376 | tf_op jit(solution)/shard_map/gather | solution.py:404
  6.9 1.4 %reshape.53 = bf16[32,6,16,16]{3,2,1,0:T(8,128)(2,1)} reshape(bf16[192,256]{1,0:T(8,128)(2,1)S(1)} %gather_fusion) | data formatting | bytes 196608 | tf_op jit(solution)/shard_map/reshape | solution.py:404
  8.3 0.0 copy-done
  8.3 1.6 %convolution_convert_fusion = bf16[32,6,16,128]{3,2,1,0:T(8,128)(2,1)S(1)} fusion(bf16[32,6,16,16]{3,2,1,0:T(8,128)(2,1)} %reshape.53, bf16[1,32,6,16,128]{4,3,2,1,0:T(8,128)(2,1)S(1)} %copy-done), kind=kOutput, calls=%fused_computation.1 | convolution fusion | flops 12976128 | bytes 1671168 | tf_op jit(solution)/shard_map/dkjc,dkjp->dkcp/dot_general | solution.py:405
  9.9 0.0 copy-done.1
  9.9 27.3 %shard_map.94 = (bf16[32,96,128]{2,1,0:T(8,128)(2,1)S(1)}, s32[32,1,128]{2,1,0:T(1,128)S(1)}, bf16[16,16,1024]{2,1,0:T(8,128)(2,1)S(1)}) custom-call(bf16[32,96,128]{2,1,0:T(8,128)(2,1)S(1)} %bitcast.23, s32[32,1,128]{2,1,0:T(1,128)S(1)} %bitcast.24, bf16[16,64,1024]{2,1,0:T(8,128)(2,1)S(1)} %copy-done.1, bf16[48,192]{1,0:T(8,128)(2,1)S(1)} %reshape.56.wb), custom_call_target="tpu_custom_call" | custom-call | tf_op jit(solution)/shard_map/pallas_call | solution.py:416
  37.2 1.7 %shard_map.95.x = bf16[16,16,1024]{2,1,0:T(8,128)(2,1)S(1)} custom-call(s32[32,1,128]{2,1,0:T(1,128)S(1)} %get-tuple-element.8.tgt, bf16[32,96,128]{2,1,0:T(8,128)(2,1)S(1)} %get-tuple-element.9.arr), custom_call_target="tpu_custom_call" | custom-call | tf_op jit(solution)/shard_map/pallas_call | solution.py:435
  38.9 22.1 %shard_map.96 = (bf16[16,64,1024]{2,1,0:T(8,128)(2,1)S(1)}, f32[4,16,144]{2,1,0:T(8,128)S(1)}) custom-call(bf16[16,16,1024]{2,1,0:T(8,128)(2,1)S(1)} %shard_map.95.x, bf16[16,64,1024]{2,1,0:T(8,128)(2,1)S(1)} %copy-done.1, bf16[64,144]{1,0:T(8,128)(2,1)S(1)} %copy.19.wf), custom_call_target="tpu_custom_call" | custom-call | tf_op jit(solution)/shard_map/pallas_call | solution.py:445
  61.0 0.0 copy-start.2
  61.0 1.3 %copy-done.2 = bf16[16,64,1024]{2,1,0:T(8,128)(2,1)} copy-done((bf16[16,64,1024]{2,1,0:T(8,128)(2,1)}, bf16[16,64,1024]{2,1,0:T(8,128)(2,1)S(1)}, u32[]{:S(2)}) %copy-start.2) | copy-done | bytes 2097176
  62.3 0.2 copy.20
  62.5 0.8 %reshape.58 = f32[64,9,16]{0,2,1:T(8,128)} reshape(f32[4,16,144]{1,0,2:T(4,128)S(1)} %copy.20) | data formatting | bytes 73728 | tf_op jit(solution)/shard_map/reshape | solution.py:470
  63.3 3.1 %copy.24 = bf16[16,64,1024]{2,1,0:T(8,128)(2,1)} copy(bf16[16,64,1024]{2,1,0:T(8,128)(2,1)} %copy-done.2) | data formatting | bytes 4194304
  66.5 0.8 %copy.25 = bf16[16,16,1024]{2,1,0:T(8,128)(2,1)} copy(bf16[16,16,1024]{2,1,0:T(8,128)(2,1)S(1)} %get-tuple-element.17) | data formatting | bytes 1048576
  (2 shorter events, 0.0 us)
Async XLA Ops:
  0.6 7.7 %copy-start = (bf16[1,32,6,16,128]{4,3,2,1,0:T(8,128)(2,1)S(1)}, bf16[1,32,6,16,128]{4,3,2,1,0:T(8,128)(2,1)}, u32[]{:S(2)}) copy-start(bf16[1,32,6,16,128]{4,3,2,1,0:T(8,128)(2,1)} %param.8) | copy-start | bytes 2359300
  4.9 5.0 %copy-start.1 = (bf16[16,64,1024]{2,1,0:T(8,128)(2,1)S(1)}, bf16[16,64,1024]{2,1,0:T(8,128)(2,1)}, u32[]{:S(2)}) copy-start(bf16[16,64,1024]{2,1,0:T(8,128)(2,1)} %g.3) | copy-start | bytes 6291460
  61.0 1.3 %copy-start.2 = (bf16[16,64,1024]{2,1,0:T(8,128)(2,1)}, bf16[16,64,1024]{2,1,0:T(8,128)(2,1)S(1)}, u32[]{:S(2)}) copy-start(bf16[16,64,1024]{2,1,0:T(8,128)(2,1)S(1)} %get-tuple-element.16) | copy-start | bytes 6291460

commit v5 on v4

--- a/solution.py
+++ b/solution.py
@@ -106,10 +106,10 @@
     packed[1] = last.astype(BF16)
 
 
-def unpack_edges(landed, padded, rows, cols, nlat):
+def unpack_edges(landed, padded, rows, cols, nlat, steps=(-1, 0, 1)):
     lat = lax.axis_index("lat")
     for k, (dr, dc) in enumerate(SIDES):
-        if dc == 0:
+        if dc == 0 or dr not in steps:
             continue
 
         def place(k=k, dr=dr, dc=dc):
@@ -294,8 +294,10 @@
     ] + edge_copies(packed, landed, hsend, hrecv, nlat, nlon)
     halo_do(halo, "start")
     own_g.wait()
-    halo_do(halo, "wait_recv")
-    unpack_edges(landed, xp, rows, cols, nlat)
+    near = [side for side in halo if side[0] == 0]
+    far = [side for side in halo if side[0] != 0]
+    halo_do(near, "wait_recv")
+    unpack_edges(landed, xp, rows, cols, nlat, (0,))
 
     def shift(r, carry):
         row = xp[r].astype(F32)
@@ -304,7 +306,7 @@
         xs[2, r] = pltpu.roll(row, width - RATE, 1)[:, EDGE : EDGE + cols].astype(BF16)
         return carry
 
-    lax.fori_loop(0, rows + 2 * RATE, shift, 0, unroll=4)
+    lax.fori_loop(RATE, rows + RATE, shift, 0, unroll=4)
 
     def taps(r):
         return jnp.concatenate(
@@ -319,7 +321,13 @@
         )
         return carry
 
-    lax.fori_loop(0, rows, grad, 0, unroll=4)
+    lax.fori_loop(RATE, rows - RATE, grad, 0, unroll=4)
+    halo_do(far, "wait_recv")
+    unpack_edges(landed, xp, rows, cols, nlat, (-1, 1))
+    lax.fori_loop(0, RATE, shift, 0, unroll=4)
+    lax.fori_loop(rows + RATE, rows + 2 * RATE, shift, 0, unroll=4)
+    lax.fori_loop(0, RATE, grad, 0, unroll=4)
+    lax.fori_loop(rows - RATE, rows, grad, 0, unroll=4)
 
     def forward(r, carry):
         feat[r] = jnp.dot(wf[...], taps(r), preferred_element_type=F32).astype(BF16)

time: 67.7 us -> 67 us (0.990)
  Pallas kernels: 51.1 us -> 50.4 us
    pallas_call x1, Pallas kernels: 22.1 us -> 21.4 us  [local(): pl.pallas_call(functools.partial(conv_kernel, nlat, nlon, scale), out_sha...]
where the time goes in v5:
time: 67 us; the launch traced here: 66.6 us
  Pallas kernels  50.4 us (75%)
  local copies, waits for them, and re-layouts  12.4 us (19%)
  matrix products  1.56 us (2%)
  other arithmetic  1.49 us (2%)
  between operations  0.72 us (1%)
    pallas_call x1, Pallas kernels, local(): pl.pallas_call(functools.partial(exchange_kernel, nlat, nlon), out_shape=...  27.3 us
    pallas_call x1, Pallas kernels, local(): pl.pallas_call(functools.partial(conv_kernel, nlat, nlon, scale), out_sha...  21.4 us
    unnamed x9, local copies, waits for them, and re-layouts  6.04 us
    gather x1, local copies, waits for them, and re-layouts, local(): element_rows = source_elements[chosen].reshape(owners, cap, points, nvars)  2 us
    pallas_call x1, Pallas kernels, local(): pl.pallas_call(functools.partial(scatter_kernel, cap), out_shape=jax.Shap...  1.7 us
    dot_general x1, matrix products, local(): jnp.einsum('dkjc,dkjp->dkcp', element_rows, local_weights, preferred_elem...  1.56 us
    reshape x1, local copies, waits for them, and re-layouts, local(): element_rows = source_elements[chosen].reshape(owners, cap, points, nvars)  1.43 us

profile of v5, /device:TPU:0, one launch (start us, length us, event | category | flops | bytes accessed | tf_op | source)
XLA Modules:
  0.0 66.6 jit_solution(11302686994927480437)
XLA Ops:
  0.6 0.0 copy-start
  0.6 0.8 %compare_select_fusion = s32[32,6,1]{0,2,1:T(1,128)S(1)} fusion(s32[1,32,6]{1,0,2:T(1,128)} %param.9), kind=kLoop, calls=%fused_computation.3 | loop fusion | flops 576 | bytes 1536 | tf_op jit(solution)/shard_map/select_n | solution.py:412
  1.4 0.1 copy.15
  1.5 0.1 reshape.61
  1.6 0.8 %copy.17 = s32[1,32,6]{2,1,0:T(8,128)S(1)} copy(s32[1,32,6]{1,0,2:T(1,128)} %param.10) | data formatting | bytes 1536 | tf_op args[3]
  2.4 0.7 %bitcast_select_fusion = s32[32,6]{1,0:T(8,128)S(1)} fusion(s32[1,32,6]{2,1,0:T(8,128)S(1)} %copy.17, s32[32]{0:T(128)} %bitcast.28), kind=kLoop, calls=%fused_computation.4 | loop fusion | flops 384 | bytes 1664 | tf_op jit(solution)/shard_map/jit(_where)/select_n | solution.py:418
  3.1 0.8 %copy.19.wf = bf16[64,144]{1,0:T(8,128)(2,1)S(1)} copy(bf16[64,144]{0,1:T(8,128)(2,1)} %bitcast.25) | data formatting | bytes 36864 | tf_op jit(solution)/shard_map/reshape | solution.py:422
  4.0 0.8 %copy.18 = bf16[3,16,3,64]{3,2,1,0:T(4,128)(2,1)S(1)} copy(bf16[3,16,3,64]{3,1,0,2:T(8,128)(2,1)} %bitcast.26) | data formatting | bytes 36864 | tf_op jit(solution)/shard_map/transpose | solution.py:421
  4.8 0.1 reshape.56.wb
  4.9 0.0 copy-start.1
  4.9 2.0 %gather_fusion = bf16[192,256]{1,0:T(8,128)(2,1)S(1)} fusion(bf16[512,256]{1,0:T(8,128)(2,1)} %param.7, s32[1024]{0:T(1024)S(1)} %pad_clamp_fusion), kind=kCustom, calls=%fused_computation | custom fusion | bytes 197376 | tf_op jit(solution)/shard_map/gather | solution.py:412
  6.9 1.4 %reshape.53 = bf16[32,6,16,16]{3,2,1,0:T(8,128)(2,1)} reshape(bf16[192,256]{1,0:T(8,128)(2,1)S(1)} %gather_fusion) | data formatting | bytes 196608 | tf_op jit(solution)/shard_map/reshape | solution.py:412
  8.3 0.0 copy-done
  8.3 1.6 %convolution_convert_fusion = bf16[32,6,16,128]{3,2,1,0:T(8,128)(2,1)S(1)} fusion(bf16[32,6,16,16]{3,2,1,0:T(8,128)(2,1)} %reshape.53, bf16[1,32,6,16,128]{4,3,2,1,0:T(8,128)(2,1)S(1)} %copy-done), kind=kOutput, calls=%fused_computation.1 | convolution fusion | flops 12976128 | bytes 1671168 | tf_op jit(solution)/shard_map/dkjc,dkjp->dkcp/dot_general | solution.py:413
  9.9 0.0 copy-done.1
  9.9 27.3 %shard_map.94 = (bf16[32,96,128]{2,1,0:T(8,128)(2,1)S(1)}, s32[32,1,128]{2,1,0:T(1,128)S(1)}, bf16[16,16,1024]{2,1,0:T(8,128)(2,1)S(1)}) custom-call(bf16[32,96,128]{2,1,0:T(8,128)(2,1)S(1)} %bitcast.23, s32[32,1,128]{2,1,0:T(1,128)S(1)} %bitcast.24, bf16[16,64,1024]{2,1,0:T(8,128)(2,1)S(1)} %copy-done.1, bf16[48,192]{1,0:T(8,128)(2,1)S(1)} %reshape.56.wb), custom_call_target="tpu_custom_call" | custom-call | tf_op jit(solution)/shard_map/pallas_call | solution.py:424
  37.2 1.7 %shard_map.95.x = bf16[16,16,1024]{2,1,0:T(8,128)(2,1)S(1)} custom-call(s32[32,1,128]{2,1,0:T(1,128)S(1)} %get-tuple-element.8.tgt, bf16[32,96,128]{2,1,0:T(8,128)(2,1)S(1)} %get-tuple-element.9.arr), custom_call_target="tpu_custom_call" | custom-call | tf_op jit(solution)/shard_map/pallas_call | solution.py:443
  38.9 21.4 %shard_map.96 = (bf16[16,64,1024]{2,1,0:T(8,128)(2,1)S(1)}, f32[4,16,144]{2,1,0:T(8,128)S(1)}) custom-call(bf16[16,16,1024]{2,1,0:T(8,128)(2,1)S(1)} %shard_map.95.x, bf16[16,64,1024]{2,1,0:T(8,128)(2,1)S(1)} %copy-done.1, bf16[64,144]{1,0:T(8,128)(2,1)S(1)} %copy.19.wf), custom_call_target="tpu_custom_call" | custom-call | tf_op jit(solution)/shard_map/pallas_call | solution.py:453
  60.3 0.0 copy-start.2
  60.4 1.3 %copy-done.2 = bf16[16,64,1024]{2,1,0:T(8,128)(2,1)} copy-done((bf16[16,64,1024]{2,1,0:T(8,128)(2,1)}, bf16[16,64,1024]{2,1,0:T(8,128)(2,1)S(1)}, u32[]{:S(2)}) %copy-start.2) | copy-done | bytes 2097176
  61.7 0.2 copy.20
  61.8 0.8 %reshape.58 = f32[64,9,16]{0,2,1:T(8,128)} reshape(f32[4,16,144]{1,0,2:T(4,128)S(1)} %copy.20) | data formatting | bytes 73728 | tf_op jit(solution)/shard_map/reshape | solution.py:478
  62.6 3.1 %copy.24 = bf16[16,64,1024]{2,1,0:T(8,128)(2,1)} copy(bf16[16,64,1024]{2,1,0:T(8,128)(2,1)} %copy-done.2) | data formatting | bytes 4194304
  65.8 0.8 %copy.25 = bf16[16,16,1024]{2,1,0:T(8,128)(2,1)} copy(bf16[16,16,1024]{2,1,0:T(8,128)(2,1)S(1)} %get-tuple-element.17) | data formatting | bytes 1048576
  (2 shorter events, 0.0 us)
Async XLA Ops:
  0.6 7.7 %copy-start = (bf16[1,32,6,16,128]{4,3,2,1,0:T(8,128)(2,1)S(1)}, bf16[1,32,6,16,128]{4,3,2,1,0:T(8,128)(2,1)}, u32[]{:S(2)}) copy-start(bf16[1,32,6,16,128]{4,3,2,1,0:T(8,128)(2,1)} %param.8) | copy-start | bytes 2359300
  4.9 5.0 %copy-start.1 = (bf16[16,64,1024]{2,1,0:T(8,128)(2,1)S(1)}, bf16[16,64,1024]{2,1,0:T(8,128)(2,1)}, u32[]{:S(2)}) copy-start(bf16[16,64,1024]{2,1,0:T(8,128)(2,1)} %g.3) | copy-start | bytes 6291460
  60.3 1.3 %copy-start.2 = (bf16[16,64,1024]{2,1,0:T(8,128)(2,1)}, bf16[16,64,1024]{2,1,0:T(8,128)(2,1)S(1)}, u32[]{:S(2)}) copy-start(bf16[16,64,1024]{2,1,0:T(8,128)(2,1)S(1)} %get-tuple-element.16) | copy-start | bytes 6291460
